TPU v7x, 256 devices: a whole 4x4x8 slice. The times are simulated.
256 devices in a mesh: bead: 32 (over z_hi, x, core), dom: 8 (over y, z_lo).
Axes of the slice: x: 4, y: 4, z: 8 (z_hi: 4, z_lo: 2; z = z_hi * 2 + z_lo), core: 2. Of those that a mesh axis runs over, the one named last changes fastest.
Arguments:
- positions: float32 [3, 32, 4096], P(None, 'bead', 'dom'), may hold values from -2.5 to 2.5
- momenta: float32 [3, 32, 4096], P(None, 'bead', 'dom'), may hold values from -6 to 6
- forces: float32 [3, 32, 4096], P(None, 'bead', 'dom'), may hold values from -6 to 6
- masses: float32 [4096], P('dom'), may hold values from 1 to 16
- charges: float32 [4096], P('dom'), may hold values from -1 to 1
- embedding: bfloat16 [4096, 240], P('dom'), may hold values from -6 to 6
- neighbours: int32 [8, 4096], P(None, 'dom'), may hold values from 0 to 895
- send_rows: int32 [3072], P('dom'), may hold values from 0 to 511
- wavevectors: int32 [3, 16384], replicated, may hold values from -12 to 12, as said below
- radial_weight: bfloat16 [2, 16, 240], replicated, may hold values from -1.5 to 1.5
- mix_weight: bfloat16 [2, 240, 240], replicated, may hold values from -0.375 to 0.375
- update_weight: bfloat16 [2, 240, 240], replicated, may hold values from -0.375 to 0.375
- readout_weight: bfloat16 [240, 240], replicated, may hold values from -0.375 to 0.375
- energy_weight: float32 [240], replicated, may hold values from -0.375 to 0.375
Outputs:
- next_positions: float32 [3, 32, 4096], P(None, 'bead', 'dom')
- next_momenta: float32 [3, 32, 4096], P(None, 'bead', 'dom')
- next_forces: float32 [3, 32, 4096], P(None, 'bead', 'dom')
Inputs may be any that keep to these rules, and one draw needn't show every extreme that they name: `wavevectors`: no component is zero.
All inputs are finite; a program needn't handle non-finite values.
Results may differ from a plain program's by a relative error of at most 0.0065.
Values may be sent and summed in bfloat16 or wider, within the bound.
A program may use at most 64 MiB of HBM per device.

v0:
```python
import math
import jax
import jax.numpy as jnp
from jax import lax
from jax.sharding import PartitionSpec as P

step_dt = 0.25
omega_cycle = 1.6
box_length = 4.0
ewald_sigma = 0.002
ewald_gain = 48.0
norm_eps = 1e-06
peak_frequency = lax.Precision.HIGHEST


def extended(cells, sides, width):
    for axis, dim in sides:
        count = lax.axis_size(axis)
        head = lax.slice_in_dim(cells, 0, width, axis=dim)
        tail = lax.slice_in_dim(cells, cells.shape[dim] - width, cells.shape[dim], axis=dim)
        cells = jnp.concatenate(
            [
                lax.ppermute(tail, axis, [(i, (i + 1) % count) for i in range(count)]),
                cells,
                lax.ppermute(head, axis, [((i + 1) % count, i) for i in range(count)]),
            ],
            axis=dim,
        )
    return cells


def mode_matrix(length):
    row_index = jnp.arange(length, dtype=jnp.int32)[:, None]
    column_index = jnp.arange(length, dtype=jnp.int32)[None, :]
    angles = 2.0 * math.pi / length * (row_index * column_index % length).astype(jnp.float32)
    single_norm = math.sqrt(1.0 / length)
    double_norm = math.sqrt(2.0 / length)
    parity = (1 - 2 * (row_index % 2)).astype(jnp.float32)
    middle = length // 2
    normal_transform = jnp.where(
        column_index == 0,
        single_norm,
        jnp.where(
            column_index < middle,
            double_norm * jnp.cos(angles),
            jnp.where(column_index == middle, single_norm * parity, double_norm * jnp.sin(angles)),
        ),
    )
    return normal_transform


def propagate(normal_mode_positions, normal_mode_momentum, masses):
    length = normal_mode_positions.shape[1]
    orders = jnp.arange(length, dtype=jnp.float32)
    omegas = 2.0 * omega_cycle * jnp.sin(math.pi * orders / length)
    cosine = jnp.cos(omegas * step_dt)[:, None]
    sines = jnp.sin(omegas * step_dt)
    omega_safe = jnp.where(orders == 0.0, 1.0, omegas)
    drift = jnp.where(orders == 0.0, step_dt, sines / omega_safe)[:, None]
    spring = (omegas * sines)[:, None]
    next_coords = cosine * normal_mode_positions + drift * normal_mode_momentum / masses
    next_moment = cosine * normal_mode_momentum - spring * masses * normal_mode_positions
    return (next_coords, next_moment)


def ewald_coef(reciprocal, atom_total):
    square = jnp.sum(reciprocal * reciprocal, 0)
    return (
        ewald_gain
        / math.sqrt(reciprocal.shape[1] * atom_total)
        * jnp.exp(-ewald_sigma * square)
        / square
    )


def phase_sums(reciprocal, centre, charge):
    phases = jnp.dot(reciprocal.T, centre, precision=peak_frequency)
    return (
        jnp.dot(jnp.cos(phases), charge, precision=peak_frequency),
        jnp.dot(jnp.sin(phases), charge, precision=peak_frequency),
    )


def ewald_force(reciprocal, centre, charge, cosine_sum, sine_sum, damping):
    phases = jnp.dot(reciprocal.T, centre, precision=peak_frequency)
    weight = (damping * cosine_sum)[:, None] * jnp.sin(phases) - (damping * sine_sum)[
        :, None
    ] * jnp.cos(phases)
    return 2.0 * charge * jnp.dot(reciprocal, weight, precision=peak_frequency)


def long_range(reciprocal, centre, charge, damping):
    cosine_part, sine_part = phase_sums(reciprocal, centre, charge)
    cosine_sum, sine_sum = lax.psum((cosine_part, sine_part), ("bead", "dom"))
    return ewald_force(reciprocal, centre, charge, cosine_sum, sine_sum, damping)


def advance(normal_mode_entries, mass_share, charge_share, reciprocal, damping):
    normal_mode_positions, normal_mode_momentum = propagate(
        normal_mode_entries[:3], normal_mode_entries[3:], mass_share
    )
    centre = normal_mode_positions[:, 0, :] / math.sqrt(normal_mode_entries.shape[1])
    long_force = long_range(reciprocal, centre, charge_share, damping)
    return (jnp.concatenate([normal_mode_positions, normal_mode_momentum], 0), long_force)


def layer_apply(
    hidden_own,
    extended_rows,
    extended_coords,
    neighbour_table,
    radial,
    mixing,
    update,
    radial_rates,
):
    owned_count = hidden_own.shape[0]
    owners = extended_coords[:, :owned_count]
    others = extended_coords[:, neighbour_table]
    offset = others - owners[:, None, :]
    distance = jnp.sum(offset * offset, 0)
    basis = (1.0 / (1.0 + radial_rates[:, None, None] * distance[None])).astype(jnp.bfloat16)
    edge_weight = jnp.einsum("mka,mf->kaf", basis, radial, preferred_element_type=jnp.float32)
    message = jnp.sum(edge_weight * extended_rows[neighbour_table], 0)
    scaled = message * lax.rsqrt(jnp.mean(message * message, -1, keepdims=True) + norm_eps)
    gated = jax.nn.silu(
        jnp.dot(scaled.astype(jnp.bfloat16), mixing, preferred_element_type=jnp.float32)
    ).astype(jnp.bfloat16)
    return hidden_own + jnp.dot(gated, update, preferred_element_type=jnp.float32)


def readout(hidden, readout_weight, energy_weight):
    activation = jax.nn.silu(
        jnp.dot(hidden.astype(jnp.bfloat16), readout_weight, preferred_element_type=jnp.float32)
    )
    return jnp.sum(activation * energy_weight)


def short_forces(
    coords,
    embedding,
    neighbours,
    send_rows,
    radial_weight,
    mix_weight,
    update_weight,
    readout_weight,
    energy_weight,
):
    owned_rows = coords.shape[2]
    ghost_rows = send_rows.shape[0] // 2
    to_before = send_rows[:ghost_rows]
    to_after = send_rows[ghost_rows:]
    radial_rates = 0.125 * 2.0 ** (0.5 * jnp.arange(radial_weight.shape[1], dtype=jnp.float32))
    apply_layer = jax.vmap(layer_apply, in_axes=(0, 0, 0, None, None, None, None, None))
    beside_all = extended(coords[:, :, send_rows], (("dom", 2),), ghost_rows)
    extended_coords = jnp.concatenate(
        [coords, beside_all[:, :, :ghost_rows], beside_all[:, :, 3 * ghost_rows :]], 2
    )
    extended_coords = jnp.moveaxis(extended_coords, 1, 0)
    hidden = embedding.astype(jnp.float32)[None]
    stored = []
    for number in range(mix_weight.shape[0]):
        rounded = hidden.astype(jnp.bfloat16)
        arrived = extended(rounded[:, send_rows, :], (("dom", 1),), ghost_rows)
        extended_rows = jnp.concatenate(
            [rounded, arrived[:, :ghost_rows], arrived[:, 3 * ghost_rows :]], 1
        ).astype(jnp.float32)
        stored.append((hidden, extended_rows))
        hidden = apply_layer(
            hidden,
            extended_rows,
            extended_coords,
            neighbours,
            radial_weight[number],
            mix_weight[number],
            update_weight[number],
            radial_rates,
        )
    cotan = jax.vmap(jax.grad(readout), in_axes=(0, None, None))(
        hidden, readout_weight, energy_weight
    )
    position_grad = jnp.zeros_like(extended_coords)
    for number in reversed(range(mix_weight.shape[0])):
        layer_input, extended_rows = stored[number]

        def local_layer(hidden_part, rows_part, coords_part):
            return apply_layer(
                hidden_part,
                rows_part,
                coords_part,
                neighbours,
                radial_weight[number],
                mix_weight[number],
                update_weight[number],
                radial_rates,
            )

        unused, pullback = jax.vjp(local_layer, layer_input, extended_rows, extended_coords)
        input_grad, feature_grad, position_part = pullback(cotan)
        position_grad = position_grad + position_part
        if number > 0:
            returned = extended(
                feature_grad[:, owned_rows:, :].astype(jnp.bfloat16), (("dom", 1),), ghost_rows
            ).astype(jnp.float32)
            owned_grad = (
                feature_grad[:, :owned_rows, :]
                .at[:, to_before, :]
                .add(returned[:, :ghost_rows])
                .at[:, to_after, :]
                .add(returned[:, 3 * ghost_rows :])
            )
            cotan = input_grad + owned_grad.astype(jnp.bfloat16).astype(jnp.float32)
    returned = extended(position_grad[:, :, owned_rows:], (("dom", 2),), ghost_rows)
    owned_force = (
        position_grad[:, :, :owned_rows]
        .at[:, :, to_before]
        .add(returned[:, :, :ghost_rows])
        .at[:, :, to_after]
        .add(returned[:, :, 3 * ghost_rows :])
    )
    return -jnp.moveaxis(owned_force, 0, 1)


def local(
    positions,
    momenta,
    forces,
    masses,
    charges,
    embedding,
    neighbours,
    send_rows,
    wavevectors,
    radial_weight,
    mix_weight,
    update_weight,
    readout_weight,
    energy_weight,
):
    beads_here = positions.shape[1]
    atom_count = positions.shape[2]
    bead_devices = lax.axis_size("bead")
    bead_slot = lax.axis_index("bead")
    bead_count = beads_here * bead_devices
    atom_share = atom_count // bead_devices
    normal_transform = mode_matrix(bead_count)
    bead_rows = lax.dynamic_slice_in_dim(normal_transform, bead_slot * beads_here, beads_here, 0)
    mass_share = lax.dynamic_slice_in_dim(masses, bead_slot * atom_share, atom_share, 0)
    charge_share = lax.dynamic_slice_in_dim(charges, bead_slot * atom_share, atom_share, 0)
    reciprocal = wavevectors.astype(jnp.float32) * (2.0 * math.pi / box_length)
    damping = ewald_coef(reciprocal, atom_count * lax.axis_size("dom"))
    coords_now, moment_now, force_now = (positions, momenta, forces)
    kicked = moment_now + 0.5 * step_dt * force_now
    stacked_arrays = jnp.concatenate([coords_now, kicked], 0)
    segment = stacked_arrays
    summed = lax.psum_scatter(
        jnp.einsum("bk,cba->ack", bead_rows, segment, precision=peak_frequency),
        "bead",
        scatter_dimension=0,
        tiled=True,
    )
    normal_mode_entries = jnp.transpose(summed, (1, 2, 0))
    joined, long_force = advance(normal_mode_entries, mass_share, charge_share, reciprocal, damping)
    packed = jnp.concatenate(
        [jnp.transpose(joined, (2, 0, 1)).reshape(atom_share, 6 * bead_count), long_force.T], 1
    )
    segment = lax.all_gather(packed, "bead", axis=0, tiled=True)
    row_count = segment.shape[0]
    coords = segment[:, : 6 * bead_count].reshape(row_count, 6, bead_count)
    restored = jnp.einsum("bk,ack->cba", bead_rows, coords, precision=peak_frequency)
    spread = segment[:, 6 * bead_count :].T[:, None, :]
    arrived = jnp.concatenate([restored, spread], 0)
    coords_now = arrived[:3]
    short_force = short_forces(
        coords_now,
        embedding,
        neighbours,
        send_rows,
        radial_weight,
        mix_weight,
        update_weight,
        readout_weight,
        energy_weight,
    )
    force_now = short_force + arrived[6:]
    moment_now = arrived[3:6] + 0.5 * step_dt * force_now
    return (coords_now, moment_now, force_now)


def solution(mesh):
    placed = (
        P(None, "bead", "dom"),
        P(None, "bead", "dom"),
        P(None, "bead", "dom"),
        P("dom"),
        P("dom"),
        P("dom", None),
        P(None, "dom"),
        P("dom"),
        P(),
        P(),
        P(),
        P(),
        P(),
        P(),
    )
    return jax.shard_map(
        local,
        mesh=mesh,
        in_specs=placed,
        out_specs=(P(None, "bead", "dom"), P(None, "bead", "dom"), P(None, "bead", "dom")),
        check_vma=False,
    )
```

profile of v0, /device:TPU:2, one launch (start us, length us, event | category | flops | bytes accessed | tf_op | source)
XLA Modules:
  0.0 636.9 jit_solution(1569555388232173794)
XLA Ops:
  7.3 0.8 multiply_add_fusion
  10.3 2.0 multiply_bitcast_fusion
  12.5 2.1 gather_fusion.2
  14.6 4.4 collective-permute-start.3
  21.1 85.0 %reduce-scatter.2.cloned.1.call-done = f32[16,6,32]{2,1,0:T(8,128)} async-done(((f32[512,6,32]{2,1,0:T(8,128)}), f32[16,6,32]{2,1,0:T(8,128)}) %reduce-scatter.2.cloned.1.call-update) | async-done | bytes 12304 | tf_op jit(solution)/shard_map/reduce_scatter | solution.py:257
  106.0 0.8 copy.158
  107.1 8.0 %fusion.207 = (f32[16384,16]{0,1:T(8,128)S(1)}, f32[16384,16]{0,1:T(8,128)S(1)}) fusion(f32[3,16]{1,0:T(4,128)S(1)} %fusion.160, s32[3,16384]{1,0:T(4,128)S(1)} %copy-done.11), kind=kOutput, calls=%fused_computation.258 | convolution fusion | flops 9535488 | bytes 2293952 | tf_op jit(solution)/shard_map/dot_general | solution.py:77
  115.0 1.3 fusion.186
  116.3 1.3 fusion.188
  117.8 240.3 %all-reduce.5.cloned.1.call-done = (f32[16384]{0:T(1024)}, f32[16384]{0:T(1024)}) async-done(((f32[16384]{0:T(1024)}, f32[16384]{0:T(1024)}), (f32[16384]{0:T(1024)}, f32[16384]{0:T(1024)})) %all-reduce.5.cloned.1.call-update) | async-done | bytes 131088 | tf_op jit(solution)/shard_map/psum | solution.py:94
  358.1 0.9 fusion.168
  359.0 1.4 convolution_multiply_fusion
  360.6 41.0 %all_gather.3 = f32[512,195]{1,0:T(8,128)S(1)} all-gather(f32[16,195]{1,0:T(8,128)S(1)} %pad_maximum_fusion.5), channel_id=1, replica_groups=mesh['bead'=32,'dom'=8] {'bead'}, dimensions={0}, use_global_device_ids=true | all-gather | bytes 411840 | tf_op jit(solution)/shard_map/all_gather | solution.py:268
  402.3 1.1 gather_fusion
  403.5 1.9 collective-permute-start.1
  406.1 16.1 %gather_fusion.3 = f32[4096,240]{1,0:T(8,128)} fusion(f32[896,240]{1,0:T(8,128)S(1)} %fusion.95, s32[4096]{0:T(1024)S(1)} %broadcast_clamp_fusion), kind=kCustom, calls=%fused_computation.3 | custom fusion | bytes 7880704 | tf_op jit(solution)/shard_map/vmap()/gather | solution.py:124
  422.2 5.3 copy.144
  427.5 5.3 copy.134
  433.6 10.8 %gather_fusion.1 = f32[4096,3]{1,0:T(8,128)S(1)} fusion(f32[3,896]{0,1:T(8,128)S(1)} %get-tuple-element.32, s32[4096]{0:T(1024)S(1)} %broadcast_clamp_fusion), kind=kCustom, calls=%fused_computation.1 | custom fusion | bytes 114688 | tf_op jit(solution)/shard_map/jvp(vmap())/gather | solution.py:119
  445.1 2.9 multiply_reduce_fusion.1
  448.4 1.1 fusion.213
  449.7 2.1 gather_fusion.4
  452.0 4.0 collective-permute-start.5
  456.2 2.6 fusion.124
  458.8 0.9 collective-permute-done.5
  459.8 3.4 collective-permute-done.4
  463.2 1.0 fusion.98
  464.2 1.5 copy.137
  465.7 16.1 %gather_fusion.5 = f32[4096,240]{1,0:T(8,128)} fusion(f32[896,240]{1,0:T(8,128)S(1)} %copy.137, s32[4096]{0:T(1024)S(1)} %broadcast_clamp_fusion), kind=kCustom, calls=%fused_computation.5 | custom fusion | bytes 7880704 | tf_op jit(solution)/shard_map/vmap()/gather | solution.py:124
  481.7 5.3 copy.139
  487.0 4.4 multiply_reduce_fusion
  491.5 1.0 fusion.106
  492.5 2.6 fusion.13
  495.1 2.1 convolution_convert_fusion.4
  497.3 2.5 multiply_reduce_fusion.4
  499.8 1.2 add_add_fusion.1
  501.7 4.7 broadcast_multiply_fusion
  506.4 5.2 copy.154
  511.6 23.1 %scatter_custom_fusion.1 = f32[896,240]{1,0:T(8,128)S(1)} fusion(s32[4096]{0:T(1024)S(1)} %bitcast.302, f32[4096,240]{1,0:T(8,128)} %bitcast.291, f32[]{:T(128)} %constant.51.clone.1), kind=kCustom, calls=%fused_computation.103 | custom fusion | flops 983040 | bytes 860672 | tf_op jit(solution)/shard_map/transpose(jvp(vmap()))/scatter-add | solution.py:124
  534.8 0.9 copy-done.12
  536.4 1.2 collective-permute-start.7
  537.5 0.8 collective-permute-start.6
  538.4 5.3 copy.140
  543.7 3.1 fusion.59
  546.8 0.8 slice_bitcast_fusion
  547.6 0.9 slice.166
  548.6 3.9 scatter_custom_fusion.2
  552.5 3.5 scatter_custom_fusion.3
  555.9 1.2 copy.143
  557.1 2.5 multiply_reduce_fusion.3
  559.7 1.2 add_add_fusion
  560.9 2.8 fusion.38
  563.7 3.1 add_multiply_fusion
  566.8 1.9 reduce_sum.128
  569.1 0.9 reduce_sum.134
  569.9 1.0 negate_bitcast_fusion
  571.7 22.8 %scatter_fusion = f32[3,896]{0,1:T(8,128)S(1)} fusion(f32[3,896]{0,1:T(8,128)S(1)} %pad_bitcast_fusion.1, s32[4096]{0:T(1024)S(1)} %bitcast.303, f32[4096,3]{1,0:T(8,128)} %bitcast.288), kind=kCustom, calls=%fused_computation.6 | custom fusion | flops 12288 | bytes 163840 | tf_op jit(solution)/shard_map/transpose(jvp(vmap()))/scatter-add | solution.py:119
  594.6 21.9 %scatter_fusion.1 = f32[3,896]{0,1:T(8,128)} fusion(f32[3,896]{0,1:T(8,128)} %pad_bitcast_fusion, s32[4096]{0:T(1024)S(1)} %bitcast.304, f32[4096,3]{1,0:T(8,128)S(1)} %bitcast.287), kind=kCustom, calls=%fused_computation.10 | custom fusion | flops 12288 | bytes 163840 | tf_op jit(solution)/shard_map/transpose(jvp(vmap()))/scatter-add | solution.py:119
  616.4 1.1 add_bitcast_fusion
  617.6 1.5 collective-permute-start.8
  619.1 2.7 collective-permute-start.9
  621.8 2.6 collective-permute-done.8
  624.4 1.8 scatter_custom_fusion.5
  626.2 1.9 scatter_custom_fusion.6
  (134 shorter events, 13.1 us)
Async XLA Ops:
  7.2 485.4 %copy-start = (bf16[240,240]{1,0:T(8,128)(2,1)S(1)}, bf16[240,240]{1,0:T(8,128)(2,1)}, u32[]{:S(2)}) copy-start(bf16[240,240]{1,0:T(8,128)(2,1)} %param.26) | copy-start | bytes 345604
  7.2 5.2 copy-start.14
  7.2 5.3 copy-start.26
  7.2 12.7 %copy-start.21 = (s32[8,512]{1,0:T(8,128)S(1)}, s32[8,512]{1,0:T(8,128)}, u32[]{:S(2)}) copy-start(s32[8,512]{1,0:T(8,128)} %param.20) | copy-start | bytes 49156
  7.2 12.7 %copy-start.27 = (f32[512]{0:T(512)S(1)}, f32[512]{0:T(512)}, u32[]{:S(2)}) copy-start(f32[512]{0:T(512)} %param.18) | copy-start | bytes 6148
  7.2 13.6 %copy-start.11 = (s32[3,16384]{1,0:T(4,128)S(1)}, s32[3,16384]{1,0:T(4,128)}, u32[]{:S(2)}) copy-start(s32[3,16384]{1,0:T(4,128)} %param.22) | copy-start | bytes 589828
  7.2 98.8 %reduce-scatter.2.cloned.1.call-start = ((), (), s32[]{:S(2)}) async-start(), calls=%async_computation.1 | async-start | bytes 2162688 | tf_op jit(solution)/shard_map/reduce_scatter | solution.py:257
  12.3 345.8 %all-reduce.5.cloned.1.call-start = ((), (), s32[]{:S(2)}) async-start(), calls=%async_computation.2 | async-start | bytes 262144 | tf_op jit(solution)/shard_map/psum | solution.py:94
  14.6 391.4 %collective-permute-start.3 = (bf16[1,192,240]{2,1,0:T(8,128)(2,1)S(1)}, bf16[1,192,240]{2,1,0:T(8,128)(2,1)S(1)}, u32[]{:S(2)}, u32[]{:S(2)}) collective-permute-start(bf16[1,192,240]{2,1,0:T(8,128)(2,1)S(1)} %get-tuple-element.38), channel_id=1, source_target_pairs={{1,0},{2,1},{3,2},{4,3},{5,4},{6,5},{7,6},{0,7},{9,8},{10,9},{11,1... | collective-permute-start | bytes 276488 | tf_op jit(solution)/shard_map/ppermute | solution.py:25
  19.1 387.0 %collective-permute-start.2 = (bf16[1,192,240]{2,1,0:T(8,128)(2,1)S(1)}, bf16[1,192,240]{2,1,0:T(8,128)(2,1)S(1)}, u32[]{:S(2)}, u32[]{:S(2)}) collective-permute-start(bf16[1,192,240]{2,1,0:T(8,128)(2,1)S(1)} %get-tuple-element.37), channel_id=1, source_target_pairs={{0,1},{1,2},{2,3},{3,4},{4,5},{5,6},{6,7},{7,0},{8,9},{9,10},{10,1... | collective-permute-start | bytes 276488 | tf_op jit(solution)/shard_map/ppermute | solution.py:23
  19.3 425.8 %copy-start.22 = (f32[16]{0:T(128)}, f32[16]{0:T(128)S(1)}, u32[]{:S(2)}) copy-start(f32[16]{0:T(128)S(1)} %power_multiply_fusion) | copy-start | bytes 196
  401.6 4.4 copy-start.6
  402.3 3.8 copy-start.9
  403.5 30.0 %collective-permute-start.1 = (f32[3,1,192]{0,2,1:T(8,128)S(1)}, f32[3,1,192]{0,2,1:T(8,128)S(1)}, u32[]{:S(2)}, u32[]{:S(2)}) collective-permute-start(f32[3,1,192]{0,2,1:T(8,128)S(1)} %get-tuple-element.36), channel_id=1, source_target_pairs={{1,0},{2,1},{3,2},{4,3},{5,4},{6,5},{7,6},{0,7},{9,8},{10,9},{11,1... | collective-permute-start | bytes 6920 | tf_op jit(solution)/shard_map/ppermute | solution.py:25
  405.4 28.1 %collective-permute-start = (f32[3,1,192]{0,2,1:T(8,128)S(1)}, f32[3,1,192]{0,2,1:T(8,128)S(1)}, u32[]{:S(2)}, u32[]{:S(2)}) collective-permute-start(f32[3,1,192]{0,2,1:T(8,128)S(1)} %get-tuple-element.35), channel_id=1, source_target_pairs={{0,1},{1,2},{2,3},{3,4},{4,5},{5,6},{6,7},{7,0},{8,9},{9,10},{10,1... | collective-permute-start | bytes 6920 | tf_op jit(solution)/shard_map/ppermute | solution.py:23
  432.8 12.3 %copy-start.18 = (bf16[2,16,240]{2,1,0:T(8,128)(2,1)S(1)}, bf16[2,16,240]{2,1,0:T(8,128)(2,1)}, u32[]{:S(2)}) copy-start(bf16[2,16,240]{2,1,0:T(8,128)(2,1)} %param.23) | copy-start | bytes 46084
  444.4 3.7 copy-start.16
  444.4 3.9 copy-start.15
  444.4 3.9 copy-start.28
  448.0 1.6 copy-start.2
  448.0 8.2 %copy-start.23 = (f32[16]{0:T(128)S(1)}, f32[16]{0:T(128)}, u32[]{:S(2)}) copy-start(f32[16]{0:T(128)} %copy-done.22) | copy-start | bytes 196
  448.1 10.8 %copy-start.19 = (f32[512]{0:T(512)}, f32[512]{0:T(512)S(1)}, u32[]{:S(2)}) copy-start(f32[512]{0:T(512)S(1)} %multiply_reduce_fusion.6) | copy-start | bytes 6148
  448.4 1.2 copy-start.13
  452.0 7.8 %collective-permute-start.5 = (bf16[1,192,240]{1,2,0:T(8,128)(2,1)S(1)}, bf16[1,192,240]{1,2,0:T(8,128)(2,1)S(1)}, u32[]{:S(2)}, u32[]{:S(2)}) collective-permute-start(bf16[1,192,240]{1,2,0:T(8,128)(2,1)S(1)} %get-tuple-element.40), channel_id=1, source_target_pairs={{1,0},{2,1},{3,2},{4,3},{5,4},{6,5},{7,6},{0,7},{9,8},{10,9},{11,1... | collective-permute-start | bytes 276488 | tf_op jit(solution)/shard_map/ppermute | solution.py:25
  456.1 7.1 %collective-permute-start.4 = (bf16[1,192,240]{1,2,0:T(8,128)(2,1)S(1)}, bf16[1,192,240]{1,2,0:T(8,128)(2,1)S(1)}, u32[]{:S(2)}, u32[]{:S(2)}) collective-permute-start(bf16[1,192,240]{1,2,0:T(8,128)(2,1)S(1)} %get-tuple-element.39), channel_id=1, source_target_pairs={{0,1},{1,2},{2,3},{3,4},{4,5},{5,6},{6,7},{7,0},{8,9},{9,10},{10,1... | collective-permute-start | bytes 276488 | tf_op jit(solution)/shard_map/ppermute | solution.py:23
  487.0 4.4 copy-start.17
  491.4 3.7 copy-start.29
  500.9 0.8 copy-start.8
  534.7 3.7 copy-start.4
  534.8 0.9 copy-start.12
  536.4 12.2 %collective-permute-start.7 = (bf16[1,192,240]{2,1,0:T(8,128)(2,1)}, bf16[1,192,240]{2,1,0:T(8,128)(2,1)S(1)}, u32[]{:S(2)}, u32[]{:S(2)}) collective-permute-start(bf16[1,192,240]{2,1,0:T(8,128)(2,1)} %get-tuple-element.30), channel_id=1, source_target_pairs={{1,0},{2,1},{3,2},{4,3},{5,4},{6,5},{7,6},{0,7},{9,8},{10,9},{11,1... | collective-permute-start | bytes 276488 | tf_op jit(solution)/shard_map/ppermute | solution.py:25
  537.5 11.1 %collective-permute-start.6 = (bf16[1,192,240]{2,1,0:T(8,128)(2,1)}, bf16[1,192,240]{2,1,0:T(8,128)(2,1)}, u32[]{:S(2)}, u32[]{:S(2)}) collective-permute-start(bf16[1,192,240]{2,1,0:T(8,128)(2,1)} %get-tuple-element.29), channel_id=1, source_target_pairs={{0,1},{1,2},{2,3},{3,4},{4,5},{5,6},{6,7},{7,0},{8,9},{9,10},{10,1... | collective-permute-start | bytes 276488 | tf_op jit(solution)/shard_map/ppermute | solution.py:23
  538.4 5.3 copy-start.24
  543.7 3.1 copy-start.5
  543.7 13.4 %copy-start.3 = (f32[512,240]{0,1:T(8,128)S(1)}, f32[512,240]{0,1:T(8,128)}, u32[]{:S(2)}) copy-start(f32[512,240]{0,1:T(8,128)} %copy-done.2) | copy-start | bytes 1474564
  546.8 12.9 %copy-start.20 = (f32[512]{0:T(512)S(1)}, f32[512]{0:T(512)}, u32[]{:S(2)}) copy-start(f32[512]{0:T(512)} %copy-done.19) | copy-start | bytes 6148
  548.6 12.2 %copy-start.25 = (f32[16]{0:T(128)S(1)}, f32[16]{0:T(128)}, u32[]{:S(2)}) copy-start(f32[16]{0:T(128)} %copy-done.22) | copy-start | bytes 196
  566.8 2.2 copy-start.1
  569.0 59.0 %copy-start.7 = (f32[512,195]{1,0:T(8,128)S(1)}, f32[512,195]{1,0:T(8,128)}, u32[]{:S(2)}) copy-start(f32[512,195]{1,0:T(8,128)} %copy-done.6) | copy-start | bytes 1198084
  569.0 59.0 %copy-start.10 = (f32[1,512,6]{2,1,0:T(8,128)S(1)}, f32[1,512,6]{2,1,0:T(8,128)}, u32[]{:S(2)}) copy-start(f32[1,512,6]{2,1,0:T(8,128)} %copy-done.9) | copy-start | bytes 36868
  617.6 6.8 %collective-permute-start.8 = (f32[1,3,192]{1,2,0:T(8,128)S(1)}, f32[1,3,192]{1,2,0:T(8,128)S(1)}, u32[]{:S(2)}, u32[]{:S(2)}) collective-permute-start(f32[1,3,192]{1,2,0:T(8,128)S(1)} %get-tuple-element.28), channel_id=1, source_target_pairs={{0,1},{1,2},{2,3},{3,4},{4,5},{5,6},{6,7},{7,0},{8,9},{9,10},{10,1... | collective-permute-start | bytes 6920 | tf_op jit(solution)/shard_map/ppermute | solution.py:23
  619.1 7.2 %collective-permute-start.9 = (f32[1,3,192]{1,2,0:T(8,128)S(1)}, f32[1,3,192]{1,2,0:T(8,128)S(1)}, u32[]{:S(2)}, u32[]{:S(2)}) collective-permute-start(f32[1,3,192]{1,2,0:T(8,128)S(1)} %get-tuple-element.27), channel_id=1, source_target_pairs={{1,0},{2,1},{3,2},{4,3},{5,4},{6,5},{7,6},{0,7},{9,8},{10,9},{11,1... | collective-permute-start | bytes 6920 | tf_op jit(solution)/shard_map/ppermute | solution.py:25
Sparse Core Ops, SparseCore 0:
  12.4 93.5 reduce-scatter.1
  117.8 240.2 all-reduce.4
where the time goes:
time: 645 us; the launch traced here: 637 us
  waiting for transfers between devices  332 us (51%)
  other arithmetic  107 us (17%)
  local copies, waits for them, and re-layouts  88.1 us (14%)
  blocking collectives  41 us (6%)
  matrix products  35.9 us (6%)
  starting transfers between devices  17.5 us (3%)
  between operations  15 us (2%)
    psum x1, waiting for transfers between devices, long_range(): cosine_sum, sine_sum = lax.psum((cosine_part, sine_part), ('bead', 'dom'))  240 us
    reduce_scatter x1, waiting for transfers between devices, local(): lax.psum_scatter(jnp.einsum('bk,cba->ack', bead_rows, segment, precision=...  85 us
    gather x6, local copies, waits for them, and re-layouts, layer_apply(): message = jnp.sum(edge_weight * extended_rows[neighbour_table], 0)  53.4 us
    scatter-add x2, other arithmetic, layer_apply(): others = extended_coords[:, neighbour_table]  44.7 us
    all_gather x1, blocking collectives, local(): segment = lax.all_gather(packed, 'bead', axis=0, tiled=True)  41 us
    scatter-add x1, other arithmetic, layer_apply(): message = jnp.sum(edge_weight * extended_rows[neighbour_table], 0)  23.1 us
    ppermute x5, starting transfers between devices, extended(): lax.ppermute(head, axis, [((i + 1) % count, i) for i in range(count)])  14.3 us
  transfers between devices with their start and end apart: 12, of which 5 were waited for; matrix products, arithmetic and copies ran while one was open for 10% of the time, Pallas kernels for 0%

commit v1 on v0

--- a/solution.py
+++ b/solution.py
@@ -91,7 +91,7 @@
 
 def long_range(reciprocal, centre, charge, damping):
     cosine_part, sine_part = phase_sums(reciprocal, centre, charge)
-    cosine_sum, sine_sum = lax.psum((cosine_part, sine_part), ("bead", "dom"))
+    cosine_sum, sine_sum = lax.psum(lax.psum((cosine_part, sine_part), "dom"), "bead")
     return ewald_force(reciprocal, centre, charge, cosine_sum, sine_sum, damping)
 
 

time: 645 us -> 747 us (1.16)
  waiting for transfers between devices: 332 us -> 429 us
    psum x1 -> x2, waiting for transfers between devices: 240 us -> 337 us  [the longest x1 260 us: long_range(): lax.psum(lax.psum((cosine_part, sine_part), 'dom'), 'bead')]
  transfers between devices with their start and end apart: 12 -> 13, of which waited for: 5 -> 6; matrix products, arithmetic and copies ran while one was open for 10% -> 8% of each run, Pallas kernels for 0% -> 0%
where the time goes in v1:
time: 747 us; the launch traced here: 739 us
  waiting for transfers between devices  429 us (57%)
  other arithmetic  107 us (14%)
  local copies, waits for them, and re-layouts  88.4 us (12%)
  blocking collectives  45.2 us (6%)
  matrix products  36 us (5%)
  starting transfers between devices  19.1 us (3%)
  between operations  14.7 us (2%)
    psum x1, waiting for transfers between devices, long_range(): lax.psum(lax.psum((cosine_part, sine_part), 'dom'), 'bead')  260 us
    reduce_scatter x1, waiting for transfers between devices, local(): lax.psum_scatter(jnp.einsum('bk,cba->ack', bead_rows, segment, precision=...  85.2 us
    psum x1, waiting for transfers between devices, long_range(): lax.psum((cosine_part, sine_part), 'dom')  76.3 us
    gather x6, local copies, waits for them, and re-layouts, layer_apply(): message = jnp.sum(edge_weight * extended_rows[neighbour_table], 0)  53.6 us
    all_gather x1, blocking collectives, local(): segment = lax.all_gather(packed, 'bead', axis=0, tiled=True)  45.2 us
    scatter-add x2, other arithmetic, layer_apply(): others = extended_coords[:, neighbour_table]  44.7 us
    scatter-add x1, other arithmetic, layer_apply(): message = jnp.sum(edge_weight * extended_rows[neighbour_table], 0)  23.1 us
    ppermute x5, starting transfers between devices, extended(): lax.ppermute(head, axis, [((i + 1) % count, i) for i in range(count)])  16 us
  transfers between devices with their start and end apart: 13, of which 6 were waited for; matrix products, arithmetic and copies ran while one was open for 8% of the time, Pallas kernels for 0%

profile of v1, /device:TPU:2, one launch (start us, length us, event | category | flops | bytes accessed | tf_op | source)
XLA Modules:
  0.0 739.3 jit_solution(15376381902577727895)
XLA Ops:
  10.3 2.0 multiply_bitcast_fusion
  12.5 2.1 gather_fusion.2
  14.6 4.4 collective-permute-start.3
  20.8 85.2 %reduce-scatter.2.cloned.1.call-done = f32[16,6,32]{2,1,0:T(8,128)} async-done(((f32[512,6,32]{2,1,0:T(8,128)}), f32[16,6,32]{2,1,0:T(8,128)}) %reduce-scatter.2.cloned.1.call-update) | async-done | bytes 12304 | tf_op jit(solution)/shard_map/reduce_scatter | solution.py:257
  106.0 0.8 copy.158
  107.0 8.0 %fusion.207 = (f32[16384,16]{0,1:T(8,128)S(1)}, f32[16384,16]{0,1:T(8,128)S(1)}) fusion(f32[3,16]{1,0:T(4,128)S(1)} %fusion.160, s32[3,16384]{1,0:T(4,128)S(1)} %copy-done.11), kind=kOutput, calls=%fused_computation.258 | convolution fusion | flops 9535488 | bytes 2293952 | tf_op jit(solution)/shard_map/dot_general | solution.py:77
  115.0 1.3 fusion.186
  116.3 1.3 fusion.188
  117.9 76.3 %all-reduce.9.cloned.1.call-done = (f32[16384]{0:T(1024)}, f32[16384]{0:T(1024)}) async-done(((f32[16384]{0:T(1024)}, f32[16384]{0:T(1024)}), (f32[16384]{0:T(1024)}, f32[16384]{0:T(1024)})) %all-reduce.9.cloned.1.call-update) | async-done | bytes 131088 | tf_op jit(solution)/shard_map/psum | solution.py:94
  194.4 260.2 %all-reduce.7.cloned.1.call-done = (f32[16384]{0:T(1024)}, f32[16384]{0:T(1024)}) async-done(((f32[16384]{0:T(1024)}, f32[16384]{0:T(1024)}), (f32[16384]{0:T(1024)}, f32[16384]{0:T(1024)})) %all-reduce.7.cloned.1.call-update) | async-done | bytes 131088 | tf_op jit(solution)/shard_map/psum | solution.py:94
  454.6 0.9 fusion.168
  455.5 1.4 convolution_multiply_fusion
  457.1 45.2 %all_gather.3 = f32[512,195]{1,0:T(8,128)S(1)} all-gather(f32[16,195]{1,0:T(8,128)S(1)} %pad_maximum_fusion.5), channel_id=1, replica_groups=mesh['bead'=32,'dom'=8] {'bead'}, dimensions={0}, use_global_device_ids=true | all-gather | bytes 411840 | tf_op jit(solution)/shard_map/all_gather | solution.py:268
  503.0 1.1 gather_fusion
  504.2 3.5 collective-permute-start.1
  508.2 16.2 %gather_fusion.3 = f32[4096,240]{1,0:T(8,128)} fusion(f32[896,240]{1,0:T(8,128)S(1)} %fusion.95, s32[4096]{0:T(1024)S(1)} %broadcast_clamp_fusion), kind=kCustom, calls=%fused_computation.3 | custom fusion | bytes 7880704 | tf_op jit(solution)/shard_map/vmap()/gather | solution.py:124
  524.4 5.3 copy.144
  529.7 5.3 copy.134
  535.8 10.8 %gather_fusion.1 = f32[4096,3]{1,0:T(8,128)S(1)} fusion(f32[3,896]{0,1:T(8,128)S(1)} %get-tuple-element.34, s32[4096]{0:T(1024)S(1)} %broadcast_clamp_fusion), kind=kCustom, calls=%fused_computation.1 | custom fusion | bytes 114688 | tf_op jit(solution)/shard_map/jvp(vmap())/gather | solution.py:119
  547.3 2.9 multiply_reduce_fusion.1
  550.6 1.1 fusion.213
  551.9 2.1 gather_fusion.4
  554.2 4.2 collective-permute-start.5
  558.6 2.6 fusion.124
  561.2 0.9 collective-permute-done.5
  562.1 3.4 collective-permute-done.4
  565.5 1.0 fusion.98
  566.5 1.5 copy.137
  568.0 16.2 %gather_fusion.5 = f32[4096,240]{1,0:T(8,128)} fusion(f32[896,240]{1,0:T(8,128)S(1)} %copy.137, s32[4096]{0:T(1024)S(1)} %broadcast_clamp_fusion), kind=kCustom, calls=%fused_computation.5 | custom fusion | bytes 7880704 | tf_op jit(solution)/shard_map/vmap()/gather | solution.py:124
  584.2 5.3 copy.139
  589.5 4.4 multiply_reduce_fusion
  593.9 1.1 fusion.106
  595.0 2.6 fusion.13
  597.6 2.1 convolution_convert_fusion.4
  599.7 2.5 multiply_reduce_fusion.4
  602.2 1.2 add_add_fusion.1
  604.2 4.7 broadcast_multiply_fusion
  608.9 5.2 copy.154
  614.1 23.1 %scatter_custom_fusion.1 = f32[896,240]{1,0:T(8,128)S(1)} fusion(s32[4096]{0:T(1024)S(1)} %bitcast.302, f32[4096,240]{1,0:T(8,128)} %bitcast.291, f32[]{:T(128)} %constant.51.clone.1), kind=kCustom, calls=%fused_computation.103 | custom fusion | flops 983040 | bytes 860672 | tf_op jit(solution)/shard_map/transpose(jvp(vmap()))/scatter-add | solution.py:124
  637.3 0.9 copy-done.12
  638.9 1.2 collective-permute-start.7
  640.1 0.8 collective-permute-start.6
  640.9 5.3 copy.140
  646.2 3.1 fusion.59
  649.3 0.8 slice_bitcast_fusion
  650.2 0.9 slice.166
  651.2 3.9 scatter_custom_fusion.2
  655.0 3.5 scatter_custom_fusion.3
  658.5 1.2 copy.143
  659.7 2.5 multiply_reduce_fusion.3
  662.2 1.2 add_add_fusion
  663.4 2.8 fusion.38
  666.2 3.2 add_multiply_fusion
  669.5 1.9 reduce_sum.128
  671.7 0.9 reduce_sum.134
  672.6 1.0 negate_bitcast_fusion
  674.3 22.8 %scatter_fusion = f32[3,896]{0,1:T(8,128)S(1)} fusion(f32[3,896]{0,1:T(8,128)S(1)} %pad_bitcast_fusion.1, s32[4096]{0:T(1024)S(1)} %bitcast.303, f32[4096,3]{1,0:T(8,128)} %bitcast.288), kind=kCustom, calls=%fused_computation.6 | custom fusion | flops 12288 | bytes 163840 | tf_op jit(solution)/shard_map/transpose(jvp(vmap()))/scatter-add | solution.py:119
  697.2 21.9 %scatter_fusion.1 = f32[3,896]{0,1:T(8,128)} fusion(f32[3,896]{0,1:T(8,128)} %pad_bitcast_fusion, s32[4096]{0:T(1024)S(1)} %bitcast.304, f32[4096,3]{1,0:T(8,128)S(1)} %bitcast.287), kind=kCustom, calls=%fused_computation.10 | custom fusion | flops 12288 | bytes 163840 | tf_op jit(solution)/shard_map/transpose(jvp(vmap()))/scatter-add | solution.py:119
  719.1 1.1 add_bitcast_fusion
  720.2 1.5 collective-permute-start.8
  721.7 2.7 collective-permute-start.9
  724.4 2.6 collective-permute-done.8
  727.0 1.8 scatter_custom_fusion.5
  728.9 1.9 scatter_custom_fusion.6
  (135 shorter events, 13.8 us)
Async XLA Ops:
  7.2 587.8 %copy-start = (bf16[240,240]{1,0:T(8,128)(2,1)S(1)}, bf16[240,240]{1,0:T(8,128)(2,1)}, u32[]{:S(2)}) copy-start(bf16[240,240]{1,0:T(8,128)(2,1)} %param.26) | copy-start | bytes 345604
  7.2 5.1 copy-start.14
  7.2 5.3 copy-start.25
  7.2 12.6 %copy-start.21 = (s32[8,512]{1,0:T(8,128)S(1)}, s32[8,512]{1,0:T(8,128)}, u32[]{:S(2)}) copy-start(s32[8,512]{1,0:T(8,128)} %param.20) | copy-start | bytes 49156
  7.2 12.6 %copy-start.26 = (f32[512]{0:T(512)S(1)}, f32[512]{0:T(512)}, u32[]{:S(2)}) copy-start(f32[512]{0:T(512)} %param.18) | copy-start | bytes 6148
  7.2 98.8 %reduce-scatter.2.cloned.1.call-start = ((), (), s32[]{:S(2)}) async-start(), calls=%async_computation.1 | async-start | bytes 2162688 | tf_op jit(solution)/shard_map/reduce_scatter | solution.py:257
  7.3 99.7 %copy-start.11 = (s32[3,16384]{1,0:T(4,128)S(1)}, s32[3,16384]{1,0:T(4,128)}, u32[]{:S(2)}) copy-start(s32[3,16384]{1,0:T(4,128)} %param.22) | copy-start | bytes 589828
  12.3 181.9 %all-reduce.9.cloned.1.call-start = ((), (), s32[]{:S(2)}) async-start(), calls=%async_computation.3 | async-start | bytes 262144 | tf_op jit(solution)/shard_map/psum | solution.py:94
  14.6 493.6 %collective-permute-start.3 = (bf16[1,192,240]{2,1,0:T(8,128)(2,1)S(1)}, bf16[1,192,240]{2,1,0:T(8,128)(2,1)S(1)}, u32[]{:S(2)}, u32[]{:S(2)}) collective-permute-start(bf16[1,192,240]{2,1,0:T(8,128)(2,1)S(1)} %get-tuple-element.40), channel_id=1, source_target_pairs={{1,0},{2,1},{3,2},{4,3},{5,4},{6,5},{7,6},{0,7},{9,8},{10,9},{11,1... | collective-permute-start | bytes 276488 | tf_op jit(solution)/shard_map/ppermute | solution.py:25
  19.0 489.1 %collective-permute-start.2 = (bf16[1,192,240]{2,1,0:T(8,128)(2,1)S(1)}, bf16[1,192,240]{2,1,0:T(8,128)(2,1)S(1)}, u32[]{:S(2)}, u32[]{:S(2)}) collective-permute-start(bf16[1,192,240]{2,1,0:T(8,128)(2,1)S(1)} %get-tuple-element.39), channel_id=1, source_target_pairs={{0,1},{1,2},{2,3},{3,4},{4,5},{5,6},{6,7},{7,0},{8,9},{9,10},{10,1... | collective-permute-start | bytes 276488 | tf_op jit(solution)/shard_map/ppermute | solution.py:23
  117.6 337.0 %all-reduce.7.cloned.1.call-start = ((), (), s32[]{:S(2)}) async-start(), calls=%async_computation.2 | async-start | bytes 262144 | tf_op jit(solution)/shard_map/psum | solution.py:94
  194.2 364.3 %copy-start.22 = (f32[16]{0:T(128)}, f32[16]{0:T(128)S(1)}, u32[]{:S(2)}) copy-start(f32[16]{0:T(128)S(1)} %power_multiply_fusion) | copy-start | bytes 196
  502.3 5.9 copy-start.6
  503.0 5.2 copy-start.9
  504.2 31.6 %collective-permute-start.1 = (f32[3,1,192]{0,2,1:T(8,128)S(1)}, f32[3,1,192]{0,2,1:T(8,128)S(1)}, u32[]{:S(2)}, u32[]{:S(2)}) collective-permute-start(f32[3,1,192]{0,2,1:T(8,128)S(1)} %get-tuple-element.38), channel_id=1, source_target_pairs={{1,0},{2,1},{3,2},{4,3},{5,4},{6,5},{7,6},{0,7},{9,8},{10,9},{11,1... | collective-permute-start | bytes 6920 | tf_op jit(solution)/shard_map/ppermute | solution.py:25
  507.7 28.1 %collective-permute-start = (f32[3,1,192]{0,2,1:T(8,128)S(1)}, f32[3,1,192]{0,2,1:T(8,128)S(1)}, u32[]{:S(2)}, u32[]{:S(2)}) collective-permute-start(f32[3,1,192]{0,2,1:T(8,128)S(1)} %get-tuple-element.37), channel_id=1, source_target_pairs={{0,1},{1,2},{2,3},{3,4},{4,5},{5,6},{6,7},{7,0},{8,9},{9,10},{10,1... | collective-permute-start | bytes 6920 | tf_op jit(solution)/shard_map/ppermute | solution.py:23
  535.0 12.3 %copy-start.18 = (bf16[2,16,240]{2,1,0:T(8,128)(2,1)S(1)}, bf16[2,16,240]{2,1,0:T(8,128)(2,1)}, u32[]{:S(2)}) copy-start(bf16[2,16,240]{2,1,0:T(8,128)(2,1)} %param.23) | copy-start | bytes 46084
  546.6 3.7 copy-start.16
  546.6 3.9 copy-start.15
  546.7 3.9 copy-start.27
  550.2 1.5 copy-start.2
  550.3 10.9 %copy-start.19 = (f32[512]{0:T(512)}, f32[512]{0:T(512)S(1)}, u32[]{:S(2)}) copy-start(f32[512]{0:T(512)S(1)} %multiply_reduce_fusion.6) | copy-start | bytes 6148
  550.6 1.2 copy-start.13
  554.2 7.9 %collective-permute-start.5 = (bf16[1,192,240]{1,2,0:T(8,128)(2,1)S(1)}, bf16[1,192,240]{1,2,0:T(8,128)(2,1)S(1)}, u32[]{:S(2)}, u32[]{:S(2)}) collective-permute-start(bf16[1,192,240]{1,2,0:T(8,128)(2,1)S(1)} %get-tuple-element.42), channel_id=1, source_target_pairs={{1,0},{2,1},{3,2},{4,3},{5,4},{6,5},{7,6},{0,7},{9,8},{10,9},{11,1... | collective-permute-start | bytes 276488 | tf_op jit(solution)/shard_map/ppermute | solution.py:25
  558.4 7.1 collective-permute-start.4
  589.5 4.4 copy-start.17
  593.8 3.8 copy-start.28
  603.4 0.8 copy-start.8
  637.2 3.7 copy-start.4
  637.3 0.9 copy-start.12
  638.9 12.2 %collective-permute-start.7 = (bf16[1,192,240]{2,1,0:T(8,128)(2,1)}, bf16[1,192,240]{2,1,0:T(8,128)(2,1)S(1)}, u32[]{:S(2)}, u32[]{:S(2)}) collective-permute-start(bf16[1,192,240]{2,1,0:T(8,128)(2,1)} %get-tuple-element.32), channel_id=1, source_target_pairs={{1,0},{2,1},{3,2},{4,3},{5,4},{6,5},{7,6},{0,7},{9,8},{10,9},{11,1... | collective-permute-start | bytes 276488 | tf_op jit(solution)/shard_map/ppermute | solution.py:25
  640.1 11.1 %collective-permute-start.6 = (bf16[1,192,240]{2,1,0:T(8,128)(2,1)}, bf16[1,192,240]{2,1,0:T(8,128)(2,1)}, u32[]{:S(2)}, u32[]{:S(2)}) collective-permute-start(bf16[1,192,240]{2,1,0:T(8,128)(2,1)} %get-tuple-element.31), channel_id=1, source_target_pairs={{0,1},{1,2},{2,3},{3,4},{4,5},{5,6},{6,7},{7,0},{8,9},{9,10},{10,1... | collective-permute-start | bytes 276488 | tf_op jit(solution)/shard_map/ppermute | solution.py:23
  640.9 5.3 copy-start.23
  646.2 3.1 copy-start.5
  646.2 13.4 %copy-start.3 = (f32[512,240]{0,1:T(8,128)S(1)}, f32[512,240]{0,1:T(8,128)}, u32[]{:S(2)}) copy-start(f32[512,240]{0,1:T(8,128)} %copy-done.2) | copy-start | bytes 1474564
  649.3 12.9 %copy-start.20 = (f32[512]{0:T(512)S(1)}, f32[512]{0:T(512)}, u32[]{:S(2)}) copy-start(f32[512]{0:T(512)} %copy-done.19) | copy-start | bytes 6148
  651.1 12.3 %copy-start.24 = (f32[16]{0:T(128)S(1)}, f32[16]{0:T(128)}, u32[]{:S(2)}) copy-start(f32[16]{0:T(128)} %copy-done.22) | copy-start | bytes 196
  669.5 2.2 copy-start.1
  671.7 59.0 %copy-start.7 = (f32[512,195]{1,0:T(8,128)S(1)}, f32[512,195]{1,0:T(8,128)}, u32[]{:S(2)}) copy-start(f32[512,195]{1,0:T(8,128)} %copy-done.6) | copy-start | bytes 1198084
  671.7 59.1 %copy-start.10 = (f32[1,512,6]{2,1,0:T(8,128)S(1)}, f32[1,512,6]{2,1,0:T(8,128)}, u32[]{:S(2)}) copy-start(f32[1,512,6]{2,1,0:T(8,128)} %copy-done.9) | copy-start | bytes 36868
  720.2 6.8 collective-permute-start.8
  721.7 7.2 collective-permute-start.9
Sparse Core Ops, SparseCore 0:
  12.4 93.5 reduce-scatter.1
  117.8 76.3 all-reduce.8
  197.1 257.4 all-reduce.6
